TPU v7x, 32 devices: a whole 2x2x4 slice. The times are simulated.
32 devices in a mesh: rep: 4 (over z), fsdp: 8 (over y, x, core).
Axes of the slice: x: 2, y: 2, z: 4, core: 2. Of those that a mesh axis runs over, the one named last changes fastest.
Arguments:
- layer_input: bfloat16 [16, 1024, 768], P('rep', 'fsdp'), may hold values from -40 to 40
- positions: int32 [16, 1024], P('rep', 'fsdp'), may hold values from 0 to 1023, as said below
- cotangent: bfloat16 [16, 1024, 768], P('rep', 'fsdp'), may hold values from -6 to 6
- w_qkv: bfloat16 [768, 2304], P('fsdp'), may hold values from -4 to 4
- w_out: bfloat16 [768, 768], P('fsdp'), may hold values from -1.75 to 1.75
- w_up: bfloat16 [768, 3072], P('fsdp'), may hold values from -0.21875 to 0.21875
- w_down: bfloat16 [768, 3072], P('fsdp'), may hold values from -0.109375 to 0.109375
- ln1_gain: bfloat16 [768], P('fsdp'), may hold values from 0.5 to 1.5
- ln1_bias: bfloat16 [768], P('fsdp'), may hold values from -1.5 to 1.5
- ln2_gain: bfloat16 [768], P('fsdp'), may hold values from 0.5 to 1.5
- ln2_bias: bfloat16 [768], P('fsdp'), may hold values from -1.5 to 1.5
- qkv_bias: bfloat16 [2304], P('fsdp'), may hold values from -2.5 to 2.5
- out_bias: bfloat16 [768], P('fsdp'), may hold values from -2.5 to 2.5
- up_bias: bfloat16 [3072], P('fsdp'), may hold values from -2.5 to 2.5
- down_bias: bfloat16 [768], P('fsdp'), may hold values from -2.5 to 2.5
Outputs:
- output: bfloat16 [16, 1024, 768], P('rep', 'fsdp')
- grad_input: bfloat16 [16, 1024, 768], P('rep', 'fsdp')
- grad_w_qkv: float32 [768, 2304], P('fsdp')
- grad_w_out: float32 [768, 768], P('fsdp')
- grad_w_up: float32 [768, 3072], P('fsdp')
- grad_w_down: float32 [768, 3072], P('fsdp')
- grad_ln1_gain: float32 [768], P('fsdp')
- grad_ln1_bias: float32 [768], P('fsdp')
- grad_ln2_gain: float32 [768], P('fsdp')
- grad_ln2_bias: float32 [768], P('fsdp')
- grad_qkv_bias: float32 [2304], P('fsdp')
- grad_out_bias: float32 [768], P('fsdp')
- grad_up_bias: float32 [3072], P('fsdp')
- grad_down_bias: float32 [768], P('fsdp')
Inputs may be any that keep to these rules, and one draw needn't show every extreme that they name: positions[s, 0] is 0, and each later positions[s, t] is either 0 or positions[s, t - 1] + 1; sequence 0 is one document of 1024 tokens.
All inputs are finite; a program needn't handle non-finite values.
Results may differ from a plain program's by a relative error of at most 0.0093.
Values may be sent and summed in bfloat16 or wider, within the bound.
No kernel may reach another device: no remote copies, remote signals or barrier semaphores. Data moves between devices by JAX's collectives and lax.ppermute only.
A program may use at most 320 MiB of HBM per device.

v0:
```python
import jax
import jax.numpy as jnp
from jax import lax
from jax.sharding import PartitionSpec as P

H = 12
HD = 64
ROT = 16
EPS = 1e-05
NEG = -1e30


def norm_rows(values, gain, shift):
    mean = jnp.mean(values, axis=-1, keepdims=True)
    centred = values - mean
    spread = jnp.mean(centred * centred, axis=-1, keepdims=True)
    return centred * lax.rsqrt(spread + EPS) * gain + shift


def rotate(values, cosine, sine):
    half = ROT // 2
    head = values[..., :ROT]
    turned = jnp.concatenate([-head[..., half:], head[..., :half]], axis=-1)
    return jnp.concatenate([head * cosine + turned * sine, values[..., ROT:]], axis=-1)


def angles(positions):
    inverse = 10000.0 ** (-jnp.arange(0, ROT, 2, dtype=jnp.float32) / ROT)
    phase = positions.astype(jnp.float32)[..., None] * inverse
    phase = jnp.concatenate([phase, phase], axis=-1)[..., None, :]
    return (jnp.cos(phase), jnp.sin(phase))


def on_device(
    layer_input,
    positions,
    cotangent,
    w_qkv,
    w_out,
    w_up,
    w_down,
    ln1_gain,
    ln1_bias,
    ln2_gain,
    ln2_bias,
    qkv_bias,
    out_bias,
    up_bias,
    down_bias,
):
    seq_count, span_len, width = layer_input.shape
    shard_count = lax.axis_size("fsdp")
    shard_index = lax.axis_index("fsdp")
    row_count = seq_count * span_len
    qkv_cols = w_qkv.shape[1]
    hidden_cols = w_up.shape[1]
    vectors = (
        lax.all_gather(ln1_gain, "fsdp", axis=0, tiled=True),
        lax.all_gather(ln1_bias, "fsdp", axis=0, tiled=True),
        lax.all_gather(ln2_gain, "fsdp", axis=0, tiled=True),
        lax.all_gather(ln2_bias, "fsdp", axis=0, tiled=True),
        lax.all_gather(qkv_bias, "fsdp", axis=0, tiled=True),
        lax.all_gather(out_bias, "fsdp", axis=0, tiled=True),
        lax.all_gather(up_bias, "fsdp", axis=0, tiled=True),
        lax.all_gather(down_bias, "fsdp", axis=0, tiled=True),
    )
    gain_one, shift_one, gain_two, shift_two, bias_qkv, bias_out, bias_up, bias_down = [
        v.astype(jnp.float32) for v in vectors
    ]
    source = layer_input.reshape(row_count, width).astype(jnp.float32)
    normed_one, pull_one = jax.vjp(norm_rows, source, gain_one, shift_one)
    normed_two, pull_two = jax.vjp(norm_rows, source, gain_two, shift_two)
    input_one = normed_one.astype(jnp.bfloat16)
    input_two = normed_two.astype(jnp.bfloat16)
    pieces = (
        lax.all_gather(w_qkv, "fsdp", axis=0, tiled=True),
        lax.all_gather(w_up, "fsdp", axis=0, tiled=True),
    )
    count = pieces[0].shape[0]
    qkv_sum = jnp.dot(input_one, pieces[0], preferred_element_type=jnp.float32)
    up_sum = jnp.dot(input_two, pieces[1], preferred_element_type=jnp.float32)
    qkv_full = qkv_sum + bias_qkv
    up_full = up_sum + bias_up
    cosine, sine = angles(positions)

    def turn_all(packed):
        shaped = packed.reshape(seq_count, span_len, 3, H, HD)
        return (
            rotate(shaped[:, :, 0], cosine, sine),
            rotate(shaped[:, :, 1], cosine, sine),
            shaped[:, :, 2],
        )

    turned, pull_turn = jax.vjp(turn_all, qkv_full)
    query_low = turned[0].astype(jnp.bfloat16)
    key_low = turned[1].astype(jnp.bfloat16)
    value_low = turned[2].astype(jnp.bfloat16)
    key_flat = key_low.reshape(seq_count, span_len, width)
    value_flat = value_low.reshape(seq_count, span_len, width)
    query_index = shard_index * span_len + jnp.arange(span_len, dtype=jnp.int32)
    first_seen = query_index[None, :] - positions

    def scores_with(key_piece):
        count = key_piece.shape[1]
        keys = key_piece.reshape(seq_count, count, H, HD)
        raw = (
            jnp.einsum("sqhd,skhd->shqk", query_low, keys, preferred_element_type=jnp.float32)
            * 0.125
        )
        key_index = jnp.arange(count, dtype=jnp.int32)
        seen = (key_index[None, None, :] <= query_index[None, :, None]) & (
            key_index[None, None, :] >= first_seen[:, :, None]
        )
        return (raw, seen[:, None])

    start_top = jnp.full((seq_count, H, span_len), NEG, jnp.float32)
    raw, seen = scores_with(lax.all_gather(key_flat, "fsdp", axis=1, tiled=True))
    masked = jnp.where(seen, raw, NEG)
    new_top = jnp.maximum(start_top, jnp.max(masked, axis=-1))
    weights = jnp.where(seen, jnp.exp(masked - new_top[..., None]), 0.0)
    total = jnp.sum(weights, axis=-1)
    log_total = new_top + jnp.log(total)
    pieces = (
        lax.all_gather(key_flat, "fsdp", axis=1, tiled=True),
        lax.all_gather(value_flat, "fsdp", axis=1, tiled=True),
    )
    raw, seen = scores_with(pieces[0])
    count = pieces[1].shape[1]
    values = pieces[1].reshape(seq_count, count, H, HD)
    probs = jnp.where(seen, jnp.exp(raw - log_total[..., None]), 0.0)
    probs_low = probs.astype(jnp.bfloat16)
    residue = (probs - probs_low.astype(jnp.float32)).astype(jnp.bfloat16)
    mixed_sum = jnp.einsum("shqk,skhd->sqhd", probs_low, values, preferred_element_type=jnp.float32)
    residue_sum = jnp.einsum("shqk,skhd->sqhd", residue, values, preferred_element_type=jnp.float32)
    attended = mixed_sum.reshape(row_count, width).astype(jnp.bfloat16)
    hidden = jax.nn.gelu(up_full, approximate=False).astype(jnp.bfloat16)
    pieces = (
        lax.all_gather(w_out, "fsdp", axis=0, tiled=True),
        lax.all_gather(w_down, "fsdp", axis=0, tiled=True),
    )
    columns = jnp.einsum("rk,ck->rc", attended, pieces[0], preferred_element_type=jnp.float32)
    columns = columns + jnp.einsum(
        "rk,ck->rc", hidden, pieces[1], preferred_element_type=jnp.float32
    )
    output = (
        (source + columns + bias_out + bias_down).astype(jnp.bfloat16).reshape(layer_input.shape)
    )
    grad_out = cotangent.reshape(row_count, width)
    pieces = (
        lax.all_gather(w_out, "fsdp", axis=0, tiled=True),
        lax.all_gather(w_down, "fsdp", axis=0, tiled=True),
    )
    count = pieces[0].shape[0]
    grad_attended = jnp.dot(grad_out, pieces[0], preferred_element_type=jnp.float32)
    grad_hidden = jnp.dot(grad_out, pieces[1], preferred_element_type=jnp.float32)
    grad_mixed = grad_attended.astype(jnp.bfloat16)
    gelu_value, pull_gelu = jax.vjp(lambda v: jax.nn.gelu(v, approximate=False), up_full)
    grad_up = pull_gelu(grad_hidden)[0].astype(jnp.bfloat16)
    grad_heads = grad_mixed.reshape(seq_count, span_len, H, HD)
    carried = jnp.sum(grad_heads.astype(jnp.float32) * (mixed_sum + residue_sum), axis=-1)
    carried_rows = jnp.transpose(carried, (0, 2, 1))
    pieces = (
        lax.all_gather(key_flat, "fsdp", axis=1, tiled=True),
        lax.all_gather(value_flat, "fsdp", axis=1, tiled=True),
    )
    raw, seen = scores_with(pieces[0])
    count = pieces[0].shape[1]
    keys = pieces[0].reshape(seq_count, count, H, HD)
    values = pieces[1].reshape(seq_count, count, H, HD)
    probs = jnp.where(seen, jnp.exp(raw - log_total[..., None]), 0.0)
    probs_low = probs.astype(jnp.bfloat16)
    grad_probs = jnp.einsum(
        "sqhd,skhd->shqk", grad_heads, values, preferred_element_type=jnp.float32
    )
    grad_scores = (probs * (grad_probs - carried_rows[..., None])).astype(jnp.bfloat16)
    grad_query = jnp.einsum(
        "shqk,skhd->sqhd", grad_scores, keys, preferred_element_type=jnp.float32
    )
    key_part = jnp.einsum(
        "shqk,sqhd->skhd", grad_scores, query_low, preferred_element_type=jnp.float32
    )
    value_part = jnp.einsum(
        "shqk,sqhd->skhd", probs_low, grad_heads, preferred_element_type=jnp.float32
    )
    both = jnp.concatenate(
        [key_part.reshape(seq_count, count, width), value_part.reshape(seq_count, count, width)],
        axis=2,
    )
    key_terms = both
    grad_query, key_terms = (grad_query, key_terms)
    grad_query = grad_query * 0.125
    key_owned = lax.psum_scatter(key_terms, "fsdp", scatter_dimension=1, tiled=True)
    grad_key = key_owned[..., :width].reshape(seq_count, span_len, H, HD) * 0.125
    grad_value = key_owned[..., width:].reshape(seq_count, span_len, H, HD)
    grad_qkv = pull_turn((grad_query, grad_key, grad_value))[0].astype(jnp.bfloat16)
    pieces = (
        lax.all_gather(w_qkv, "fsdp", axis=0, tiled=True),
        lax.all_gather(w_up, "fsdp", axis=0, tiled=True),
    )
    columns_one = jnp.einsum("rk,ck->rc", grad_qkv, pieces[0], preferred_element_type=jnp.float32)
    columns_two = jnp.einsum("rk,ck->rc", grad_up, pieces[1], preferred_element_type=jnp.float32)
    grad_source_one, grad_gain_one, grad_shift_one = pull_one(columns_one)
    grad_source_two, grad_gain_two, grad_shift_two = pull_two(columns_two)
    grad_out_float = grad_out.astype(jnp.float32)
    grad_input = (
        (grad_out_float + grad_source_one + grad_source_two)
        .astype(jnp.bfloat16)
        .reshape(layer_input.shape)
    )
    grad_out_total = jnp.sum(grad_out_float, axis=0)
    local_vectors = (
        grad_gain_one,
        grad_shift_one,
        grad_gain_two,
        grad_shift_two,
        jnp.sum(grad_qkv.astype(jnp.float32), axis=0),
        grad_out_total,
        jnp.sum(grad_up.astype(jnp.float32), axis=0),
    )
    summed = lax.psum(
        (
            local_vectors[0],
            local_vectors[1],
            local_vectors[2],
            local_vectors[3],
            local_vectors[4],
            local_vectors[5],
            local_vectors[6],
        ),
        ("rep", "fsdp"),
    )
    owned_vectors = [
        lax.dynamic_slice_in_dim(
            v, shard_index * (v.shape[0] // shard_count), v.shape[0] // shard_count
        )
        for v in summed
    ]
    owned = lax.psum_scatter(
        jnp.concatenate(
            [
                jnp.einsum("rc,rk->ck", input_one, grad_qkv, preferred_element_type=jnp.float32),
                jnp.einsum("rc,rk->ck", grad_out, attended, preferred_element_type=jnp.float32),
                jnp.einsum("rc,rk->ck", input_two, grad_up, preferred_element_type=jnp.float32),
                jnp.einsum("rc,rk->ck", grad_out, hidden, preferred_element_type=jnp.float32),
            ],
            axis=1,
        ),
        "fsdp",
        scatter_dimension=0,
        tiled=True,
    )
    owned = lax.psum(owned, "rep")
    edge_two = qkv_cols + width
    edge_three = edge_two + hidden_cols
    grad_w_qkv = owned[:, :qkv_cols]
    grad_w_out = owned[:, qkv_cols:edge_two]
    grad_w_up = owned[:, edge_two:edge_three]
    grad_w_down = owned[:, edge_three:]
    return (
        output,
        grad_input,
        grad_w_qkv,
        grad_w_out,
        grad_w_up,
        grad_w_down,
        owned_vectors[0],
        owned_vectors[1],
        owned_vectors[2],
        owned_vectors[3],
        owned_vectors[4],
        owned_vectors[5],
        owned_vectors[6],
        owned_vectors[5],
    )


def solution(mesh):
    return jax.shard_map(
        on_device,
        mesh=mesh,
        in_specs=(
            P("rep", "fsdp", None),
            P("rep", "fsdp"),
            P("rep", "fsdp", None),
            P("fsdp", None),
            P("fsdp", None),
            P("fsdp", None),
            P("fsdp", None),
            P("fsdp"),
            P("fsdp"),
            P("fsdp"),
            P("fsdp"),
            P("fsdp"),
            P("fsdp"),
            P("fsdp"),
            P("fsdp"),
        ),
        out_specs=(
            P("rep", "fsdp", None),
            P("rep", "fsdp", None),
            P("fsdp", None),
            P("fsdp", None),
            P("fsdp", None),
            P("fsdp", None),
            P("fsdp"),
            P("fsdp"),
            P("fsdp"),
            P("fsdp"),
            P("fsdp"),
            P("fsdp"),
            P("fsdp"),
            P("fsdp"),
        ),
        check_vma=False,
    )
```

profile of v0, /device:TPU:0, one launch (start us, length us, event | category | flops | bytes accessed | tf_op | source)
XLA Modules:
  0.0 780.7 jit_solution(14124956346842506521)
XLA Ops:
  8.7 1.3 convert_reduce_fusion.2
  10.1 1.5 fusion.28
  12.5 1.2 dynamic-slice
  15.1 0.8 dynamic-update-slice
  15.9 0.8 dynamic-update-slice.1
  16.8 0.8 dynamic-update-slice.3
  18.4 0.8 dynamic-update-slice.5
  19.3 0.8 dynamic-update-slice.6
  20.1 0.9 dynamic-update-slice.2
  21.0 26.5 %all-reduce.19 = (bf16[768]{0:T(1024)(128)(2,1)S(1)}, bf16[768]{0:T(1024)(128)(2,1)S(1)}, bf16[768]{0:T(1024)(128)(2,1)}, bf16[768]{0:T(1024)(128)(2,1)}, bf16[7...) all-reduce(bf16[768]{0:T(1024)(128)(2,1)S(1)} %dynamic-update-slice, ...), channel_id=1, replica_groups=mesh['rep'=4,'fsdp'=8] {'fsdp'}, use_global_device_ids=true, to_apply=%add.15 | all-reduce | flops 6912 | bytes 27648
  47.6 1.6 fusion.33
  49.2 6.1 convolution_add_fusion
  55.4 6.2 copy.46
  61.5 6.3 reshape.249
  67.9 2.2 fusion.78
  70.7 1.0 copy-done.7
  71.8 1.0 pad_maximum_fusion.3
  72.9 1.7 slice.108
  74.6 1.1 copy.47
  77.7 2.9 convolution_convert_fusion
  80.6 1.5 copy.51
  82.1 1.1 reshape.254
  83.2 1.4 slice.110
  84.6 37.4 %all-gather.12.cloned.1.call-done = bf16[4,1024,768]{1,2,0:T(8,128)(2,1)} async-done(((bf16[4,128,768]{1,2,0:T(8,128)(2,1)}), bf16[4,1024,768]{1,2,0:T(8,128)(2,1)}) %all-gather.12.cloned.1.call-update) | async-done | bytes 6291472 | tf_op jit(solution)/shard_map/all_gather | solution.py:124
  121.9 12.9 %select_reduce_fusion.1 = (f32[4,12,128]{2,1,0:T(8,128)S(1)}, f32[4,12,128,1024]{3,2,1,0:T(8,128)}) fusion(pred[4,128,1024]{2,1,0:T(8,128)(4,1)S(1)} %fusion.13, bf16[4,1024,12,64]{1,3,2,0:T(8,128)(2,1)} %bitcast.164, bf16[4,128,12,48]{1,3,2,0:T(8,128)(2,1)S(1)} %slice.110, bf16[4,128,12,16]{1,3,2,0:T(8,128)(2,1)S(1)} %get-tuple-element.61), kind=kOutput, calls=%fused_computation.6 | convolution fusion | flops 825747456 | bytes 32792576 | tf_op jit(solution)/shard_map/sqhd,skhd->shqk/dot_general | solution.py:107
  134.9 12.2 %select_reduce_fusion = f32[4,12,128]{2,1,0:T(8,128)S(1)} fusion(f32[4,12,128,1024]{3,2,1,0:T(8,128)} %get-tuple-element.76, f32[4,12,128]{2,1,0:T(8,128)S(1)} %broadcast_maximum_fusion, pred[4,128,1024]{2,1,0:T(8,128)(4,1)S(1)} %fusion.13), kind=kLoop, calls=%fused_computation.5 | loop fusion | flops 31451136 | bytes 25739264 | tf_op jit(solution)/shard_map/reduce_sum | solution.py:121
  147.1 23.9 %all-gather.10.cloned.1.call-done = bf16[4,1024,768]{1,2,0:T(8,128)(2,1)} async-done(((bf16[4,128,768]{1,2,0:T(8,128)(2,1)}), bf16[4,1024,768]{1,2,0:T(8,128)(2,1)}) %all-gather.10.cloned.1.call-update) | async-done | bytes 6291472 | tf_op jit(solution)/shard_map/all_gather | solution.py:125
  170.9 14.2 %fusion.58 = f32[4,12,64,128]{3,2,1,0:T(8,128)} fusion(bf16[4,1024,12,64]{1,3,2,0:T(8,128)(2,1)} %bitcast.190, f32[4,12,128,1024]{3,2,1,0:T(8,128)} %get-tuple-element.76, f32[4,12,128]{2,1,0:T(8,128)S(1)} %log_add_fusion, pred[4,128,1024]{2,1,0:T(8,128)(4,1)S(1)} %fusion.13), kind=kOutput, calls=%fused_computation.110 | convolution fusion | flops 830472192 | bytes 33579008 | tf_op jit(solution)/shard_map/shqk,skhd->sqhd/dot_general | solution.py:133
  185.2 15.0 %fusion.16 = f32[4,128,12]{1,2,0:T(8,128)S(1)} fusion(f32[4,12,64,128]{3,2,1,0:T(8,128)} %fusion.58, bf16[4,1024,12,64]{1,3,2,0:T(8,128)(2,1)} %bitcast.191, f32[4,12,128,1024]{3,2,1,0:T(8,128)} %get-tuple-element.76, f32[4,12,128]{2,1,0:T(8,128)S(1)} %log_add_fusion, pred[4,128,1024]{2,1,0:T(8,128)(4,1)S(1)} %fusion.13, bf16[4,128,12,64]{1,0,3,2:T(4,128)(2,1)} %reshape.254), kind=kOutput, calls=%fused_computation.48 | convolution fusion | flops 850913280 | bytes 34390016 | tf_op jit(solution)/shard_map/shqk,skhd->sqhd/dot_general | solution.py:134
  200.2 20.5 %multiply_convert_fusion = bf16[4,12,128,1024]{3,2,1,0:T(8,128)(2,1)} fusion(f32[4,12,128,1024]{3,2,1,0:T(8,128)} %get-tuple-element.76, f32[4,12,128]{2,1,0:T(8,128)S(1)} %bitcast.194, f32[4,12,128]{2,1,0:T(8,128)S(1)} %log_add_fusion, pred[4,128,1024]{2,1,0:T(8,128)(4,1)S(1)} %fusion.13, bf16[4,1024,12,64]{1,3,2,0:T(8,128)(2,1)} %bitcast.192, ...), kind=kOutput, calls=%fused_computation.2 | convolution fusion | flops 843055104 | bytes 45400064 | tf_op jit(solution)/shard_map/sqhd,skhd->shqk/dot_general | solution.py:172
  220.6 11.1 %fusion.50 = f32[4,12,64,1024]{3,2,1,0:T(8,128)} fusion(bf16[4,12,128,1024]{3,2,1,0:T(8,128)(2,1)} %multiply_convert_fusion, bf16[4,128,12,48]{1,3,2,0:T(8,128)(2,1)S(1)} %slice.110, bf16[4,128,12,16]{1,3,2,0:T(8,128)(2,1)S(1)} %get-tuple-element.61), kind=kOutput, calls=%fused_computation.98 | convolution fusion | flops 806879232 | bytes 25952256 | tf_op jit(solution)/shard_map/shqk,sqhd->skhd/dot_general | solution.py:179
  231.8 14.8 %fusion.47 = f32[4,12,64,1024]{3,2,1,0:T(8,128)} fusion(bf16[4,128,12,64]{1,0,3,2:T(4,128)(2,1)S(1)} %copy-done.12, f32[4,12,128,1024]{3,2,1,0:T(8,128)} %get-tuple-element.76, f32[4,12,128]{2,1,0:T(8,128)S(1)} %log_add_fusion, pred[4,128,1024]{2,1,0:T(8,128)(4,1)S(1)} %fusion.13), kind=kOutput, calls=%fused_computation.94 | convolution fusion | flops 830472192 | bytes 39084032 | tf_op jit(solution)/shard_map/shqk,sqhd->skhd/dot_general | solution.py:182
  246.5 18.8 %pad_maximum_fusion.1 = f32[4,1024,1536]{1,2,0:T(8,128)} fusion(f32[4,1024,768]{1,2,0:T(8,128)} %bitcast.163, f32[4,1024,768]{1,2,0:T(8,128)} %bitcast.162), kind=kLoop, calls=%fused_computation.1 | loop fusion | flops 6291456 | bytes 50331648 | tf_op jit(solution)/shard_map/concatenate | solution.py:185
  266.0 9.4 %all-gather = bf16[8,1,384]{2,1,0:T(2,128)(2,1)S(1)} all-gather(bf16[1,1,384]{2,1,0:T(2,128)(2,1)S(1)} %reshape.280), channel_id=1, replica_groups=mesh['rep'=4,'fsdp'=8] {'fsdp'}, dimensions={0}, use_global_device_ids=true | all-gather | bytes 6912 | tf_op jit(solution)/shard_map/all_gather | solution.py:64
  275.5 1.2 fusion.31
  276.7 8.9 %fusion.83 = f32[512,3072]{1,0:T(8,128)} fusion(bf16[512,768]{1,0:T(8,128)(2,1)S(1)} %get-tuple-element.54, bf16[768,3072]{1,0:T(8,128)(2,1)} %all-gather.16.cloned.1.call-done), kind=kOutput, calls=%fused_computation.154 | convolution fusion | flops 2415919104 | bytes 11796480 | tf_op jit(solution)/shard_map/dot_general | solution.py:81
  285.6 19.4 %convert_reduce_fusion = (f32[3072]{0:T(1024)S(1)}, bf16[512,3072]{1,0:T(8,128)(2,1)S(1)}, f32[512,3072]{1,0:T(8,128)S(1)}) fusion(f32[512,3072]{1,0:T(8,128)} %fusion.83, f32[3072]{0:T(1024)S(1)} %bitcast.188, bf16[512,768]{1,0:T(8,128)(2,1)S(1)} %bitcast.170, bf16[768,3072]{1,0:T(8,128)(2,1)} %all-gather.18.cloned.1.call-done), kind=kOutput, calls=%fused_computation.12 | convolution fusion | flops 2533880832 | bytes 21258240 | tf_op jit(solution)/shard_map/dot_general | solution.py:155
  305.0 3.2 multiply_convert_fusion.1
  308.2 7.8 convolution_bitcast_fusion
  316.0 5.2 fusion.86
  321.2 11.3 %multiply_bitcast_fusion = f32[4,128,12,64]{1,3,2,0:T(8,128)S(1)} fusion(bf16[4,1024,12,64]{1,3,2,0:T(8,128)(2,1)} %bitcast.165, bf16[4,12,128,1024]{3,2,1,0:T(8,128)(2,1)} %multiply_convert_fusion), kind=kOutput, calls=%fused_computation.82 | convolution fusion | flops 805699584 | bytes 20447232 | tf_op jit(solution)/shard_map/shqk,skhd->sqhd/dot_general | solution.py:176
  332.5 2.3 convert_bitcast_fusion
  335.5 0.9 copy-done.9
  336.3 2.2 convolution_bitcast_fusion.1
  338.5 2.0 copy.57
  340.6 82.4 %reduce-scatter.3.cloned.1.call-done = f32[4,128,1536]{1,2,0:T(8,128)} async-done(((f32[4,1024,1536]{1,2,0:T(8,128)}), f32[4,128,1536]{1,2,0:T(8,128)}) %reduce-scatter.3.cloned.1.call-update) | async-done | bytes 3145744 | tf_op jit(solution)/shard_map/reduce_scatter | solution.py:192
  423.0 2.2 fusion.80
  427.4 2.2 copy.55
  429.7 1.5 copy-done.13
  431.2 4.9 fusion.9
  436.1 19.4 %pad_maximum_fusion = f32[768,9216]{1,0:T(8,128)} fusion(f32[768,3072]{1,0:T(8,128)} %convolution_bitcast_fusion, f32[768,3072]{1,0:T(8,128)} %fusion.86, f32[768,768]{1,0:T(8,128)S(1)} %copy.57, f32[768,2304]{1,0:T(8,128)} %fusion.9), kind=kLoop, calls=%fused_computation | loop fusion | flops 21233664 | bytes 56623104 | tf_op jit(solution)/shard_map/concatenate | solution.py:239
  456.4 172.6 %reduce-scatter.5.cloned.1.call-done = f32[96,9216]{1,0:T(8,128)} async-done(((f32[768,9216]{1,0:T(8,128)}), f32[96,9216]{1,0:T(8,128)}) %reduce-scatter.5.cloned.1.call-update) | async-done | bytes 3538960 | tf_op jit(solution)/shard_map/reduce_scatter | solution.py:238
  629.0 6.1 fusion.85
  635.1 5.8 fusion.84
  641.0 1.8 fusion.42
  642.9 5.4 fusion.76
  648.3 1.1 copy-done.6
  649.4 1.4 fusion.37
  650.8 44.4 %all-reduce.18 = (f32[768]{0:T(1024)S(1)}, f32[768]{0:T(1024)S(1)}, f32[768]{0:T(1024)S(1)}, f32[768]{0:T(1024)S(1)}, f32[2304]{0:T(1024)S(1)}, /*index=5*/f32[768]{0:T(1024)S(1)}, f32[3072]{0:T(1024)S(1)}) all-reduce(f32[768]{0:T(1024)S(1)} %get-tuple-element.23, ...), channel_id=1, replica_groups=mesh['rep'=4,'fsdp'=8] {'rep','fsdp'}, use_global_device_ids=true, to_apply=%region_13.14 | all-reduce | flops 9216 | bytes 73728 | tf_op jit(solution)/shard_map/psum | solution.py:220
  698.9 3.0 add_convert_fusion.2
  701.9 64.2 %all-reduce.22.cloned.1.call-done = f32[96,9216]{1,0:T(8,128)} async-done(((f32[96,9216]{1,0:T(8,128)}), f32[96,9216]{1,0:T(8,128)}) %all-reduce.22.cloned.1.call-update) | async-done | bytes 3538960 | tf_op jit(solution)/shard_map/psum | solution.py:252
  766.1 3.3 fusion.79
  769.4 2.1 slice.88
  771.5 1.7 slice.89
  (144 shorter events, 14.8 us)
Async XLA Ops:
  7.2 42.0 %all-gather.8.cloned.1.call-start = ((), (), s32[]{:S(2)}) async-start(), calls=%async_computation.2 | async-start | bytes 3981312 | tf_op jit(solution)/shard_map/all_gather | solution.py:76
  7.9 69.8 %all-gather.14.cloned.1.call-start = ((), (), s32[]{:S(2)}) async-start(), calls=%async_computation.5 | async-start | bytes 1327104 | tf_op jit(solution)/shard_map/all_gather | solution.py:138
  8.7 113.3 %all-gather.12.cloned.1.call-start = ((), (), s32[]{:S(2)}) async-start(), calls=%async_computation.4 | async-start | bytes 7077888 | tf_op jit(solution)/shard_map/all_gather | solution.py:124
  10.0 45.3 %copy-start.23 = (f32[512]{0:T(512)}, f32[512]{0:T(512)S(1)}, u32[]{:S(2)}) copy-start(f32[512]{0:T(512)S(1)} %get-tuple-element.73) | copy-start | bytes 6148
  11.6 263.9 %copy-start.27 = (f32[4,128]{1,0:T(4,128)}, f32[4,128]{1,0:T(4,128)S(1)}, u32[]{:S(2)}) copy-start(f32[4,128]{1,0:T(4,128)S(1)} %fusion.28) | copy-start | bytes 6148
  12.5 58.2 %copy-start.15 = (f32[4,128,16]{1,2,0:T(8,128)}, f32[4,128,16]{1,2,0:T(8,128)S(1)}, u32[]{:S(2)}) copy-start(f32[4,128,16]{1,2,0:T(8,128)S(1)} %get-tuple-element.67) | copy-start | bytes 98308
  12.5 58.2 %copy-start.17 = (f32[4,128,16]{1,2,0:T(8,128)}, f32[4,128,16]{1,2,0:T(8,128)S(1)}, u32[]{:S(2)}) copy-start(f32[4,128,16]{1,2,0:T(8,128)S(1)} %get-tuple-element.68) | copy-start | bytes 98308
  47.5 228.0 %copy-start.19 = (f32[768]{0:T(1024)}, f32[768]{0:T(1024)S(1)}, u32[]{:S(2)}) copy-start(f32[768]{0:T(1024)S(1)} %convert_element_type.126) | copy-start | bytes 9220
  47.5 7.9 %copy-start.21 = (f32[768]{0:T(1024)}, f32[768]{0:T(1024)S(1)}, u32[]{:S(2)}) copy-start(f32[768]{0:T(1024)S(1)} %convert_element_type.137) | copy-start | bytes 9220
  47.6 7.8 copy-start.25
  70.5 1.2 copy-start.7
  71.7 6.0 copy-start.5
  72.8 98.1 %all-gather.10.cloned.1.call-start = ((), (), s32[]{:S(2)}) async-start(), calls=%async_computation.3 | async-start | bytes 7077888 | tf_op jit(solution)/shard_map/all_gather | solution.py:125
  75.6 201.1 %all-gather.16.cloned.1.call-start = ((), (), s32[]{:S(2)}) async-start(), calls=%async_computation.6 | async-start | bytes 5308416 | tf_op jit(solution)/shard_map/all_gather | solution.py:77
  76.2 209.3 %all-gather.18.cloned.1.call-start = ((), (), s32[]{:S(2)}) async-start(), calls=%async_computation.7 | async-start | bytes 5308416 | tf_op jit(solution)/shard_map/all_gather | solution.py:139
  76.8 346.2 %reduce-scatter.3.cloned.1.call-start = ((), (), s32[]{:S(2)}) async-start(), calls=%async_computation.8 | async-start | bytes 28311552 | tf_op jit(solution)/shard_map/reduce_scatter | solution.py:192
  220.6 11.1 %copy-start.12 = (bf16[4,128,12,64]{1,0,3,2:T(4,128)(2,1)S(1)}, bf16[4,128,12,64]{1,0,3,2:T(4,128)(2,1)}, u32[]{:S(2)}) copy-start(bf16[4,128,12,64]{1,0,3,2:T(4,128)(2,1)} %reshape.254) | copy-start | bytes 2359300
  265.3 0.7 copy-start.31
  265.3 10.1 %copy-start = (bf16[4,128,768]{2,1,0:T(8,128)(2,1)S(1)}, bf16[4,128,768]{2,1,0:T(8,128)(2,1)}, u32[]{:S(2)}) copy-start(bf16[4,128,768]{2,1,0:T(8,128)(2,1)} %param.15) | copy-start | bytes 2359300
  265.3 363.6 %reduce-scatter.5.cloned.1.call-start = ((), (), s32[]{:S(2)}) async-start(), calls=%async_computation.9 | async-start | bytes 31850496 | tf_op jit(solution)/shard_map/reduce_scatter | solution.py:238
  285.6 19.4 %copy-start.2 = (f32[512,3072]{1,0:T(8,128)S(1)}, f32[512,3072]{1,0:T(8,128)}, u32[]{:S(2)}) copy-start(f32[512,3072]{1,0:T(8,128)} %fusion.83) | copy-start | bytes 18874372
  305.0 11.0 %copy-start.8 = (bf16[512,3072]{1,0:T(8,128)(2,1)}, bf16[512,3072]{1,0:T(8,128)(2,1)S(1)}, u32[]{:S(2)}) copy-start(bf16[512,3072]{1,0:T(8,128)(2,1)S(1)} %get-tuple-element.39) | copy-start | bytes 9437188
  332.5 3.0 copy-start.3
  335.5 0.9 copy-start.9
  338.5 86.7 %copy-start.18 = (f32[4,128,16]{1,2,0:T(8,128)S(1)}, f32[4,128,16]{1,2,0:T(8,128)}, u32[]{:S(2)}) copy-start(f32[4,128,16]{1,2,0:T(8,128)} %copy-done.17) | copy-start | bytes 98308
  340.6 85.1 %copy-start.16 = (f32[4,128,16]{1,2,0:T(8,128)S(1)}, f32[4,128,16]{1,2,0:T(8,128)}, u32[]{:S(2)}) copy-start(f32[4,128,16]{1,2,0:T(8,128)} %copy-done.15) | copy-start | bytes 98308
  423.0 2.4 copy-start.4
  425.5 1.3 slice-start
  427.0 4.2 copy-start.14
  429.7 1.5 copy-start.13
  455.5 0.7 copy-start.30
  455.5 0.7 copy-start.29
  455.5 310.6 %all-reduce.22.cloned.1.call-start = ((), (), s32[]{:S(2)}) async-start(), calls=%async_computation.10 | async-start | bytes 7077888 | tf_op jit(solution)/shard_map/psum | solution.py:252
  629.0 6.1 copy-start.11
  635.1 5.9 copy-start.1
  635.1 5.9 copy-start.10
  635.1 5.9 copy-start.32
  641.0 1.9 copy-start.20
  641.0 1.9 copy-start.22
  641.0 1.9 copy-start.24
  642.9 5.4 copy-start.28
  642.9 6.5 copy-start.26
  648.2 1.2 copy-start.6
  695.3 78.0 %copy-start.33 = (f32[96]{0:T(128)}, f32[96]{0:T(128)S(1)}, u32[]{:S(2)}) copy-start(f32[96]{0:T(128)S(1)} %dynamic_slice.26) | copy-start | bytes 1156
Sparse Core Ops, SparseCore 0:
  9.9 36.8 all-gather.7
  48.7 24.0 all-gather.13
  75.2 46.6 all-gather.11
  124.2 46.6 all-gather.9
  172.7 38.9 all-gather.15
  213.4 38.8 all-gather.17
  265.5 157.4 reduce-scatter.2
  455.7 173.2 reduce-scatter.4
  631.3 134.7 all-reduce.21
where the time goes:
time: 787 us; the launch traced here: 781 us
  waiting for transfers between devices  383 us (49%)
  matrix products  176 us (22%)
  blocking collectives  80.3 us (10%)
  other arithmetic  72.3 us (9%)
  local copies, waits for them, and re-layouts  51.7 us (7%)
  between operations  16.3 us (2%)
    reduce_scatter x1, waiting for transfers between devices, on_device(): lax.psum_scatter(jnp.concatenate([jnp.einsum('rc,rk->ck', input_one, grad...  173 us
    reduce_scatter x1, waiting for transfers between devices, on_device(): lax.psum_scatter(key_terms, 'fsdp', scatter_dimension=1, tiled=True)  82.4 us
    psum x1, waiting for transfers between devices, on_device(): owned = lax.psum(owned, 'rep')  64.2 us
    psum x1, blocking collectives, on_device(): lax.psum((local_vectors[0], local_vectors[1], local_vectors[2], local_vec...  44.4 us
    all_gather x1, waiting for transfers between devices, on_device(): lax.all_gather(key_flat, 'fsdp', axis=1, tiled=True)  37.4 us
    unnamed x1, blocking collectives  26.5 us
    all_gather x1, waiting for transfers between devices, on_device(): lax.all_gather(value_flat, 'fsdp', axis=1, tiled=True)  23.9 us
    dot_general x1, matrix products, on_device(): jnp.einsum('sqhd,skhd->shqk', grad_heads, values, preferred_element_type=...  20.5 us
  transfers between devices with their start and end apart: 9, of which 5 were waited for; matrix products, arithmetic and copies ran while one was open for 33% of the time, Pallas kernels for 0%

commit v1 on v0

--- a/solution.py
+++ b/solution.py
@@ -1,3 +1,4 @@
+import functools
 import jax
 import jax.numpy as jnp
 from jax import lax
@@ -8,6 +9,13 @@
 ROT = 16
 EPS = 1e-05
 NEG = -1e30
+
+
+def move_task(panel, net_axis):
+    return jnp.sum(lax.all_gather(panel, net_axis), axis=0)
+
+
+press_clusters_over_axis = functools.partial(move_task, net_axis="rep")
 
 
 def norm_rows(values, gain, shift):
@@ -249,7 +257,7 @@
         scatter_dimension=0,
         tiled=True,
     )
-    owned = lax.psum(owned, "rep")
+    owned = press_clusters_over_axis(owned)
     edge_two = qkv_cols + width
     edge_three = edge_two + hidden_cols
     grad_w_qkv = owned[:, :qkv_cols]

time: 787 us -> 899 us (1.14)
  waiting for transfers between devices: 383 us -> 482 us
  blocking collectives: 80.3 us -> 91 us
    all_gather x0 -> x1, waiting for transfers between devices: none -> 162 us  [move_task(): return jnp.sum(lax.all_gather(panel, net_axis), axis=0)]
    psum x1 -> x0, waiting for transfers between devices: 64.2 us -> none  [on_device(): owned = lax.psum(owned, 'rep')]
    psum x1, blocking collectives: 44.4 us -> 55 us  [on_device(): lax.psum((local_vectors[0], local_vectors[1], local_vectors[2], local_vec...]
  transfers between devices with their start and end apart: 9 -> 9, of which waited for: 5 -> 5; matrix products, arithmetic and copies ran while one was open for 33% -> 29% of each run, Pallas kernels for 0% -> 0%
where the time goes in v1:
time: 899 us; the launch traced here: 893 us
  waiting for transfers between devices  482 us (54%)
  matrix products  176 us (20%)
  blocking collectives  91 us (10%)
  other arithmetic  78.7 us (9%)
  local copies, waits for them, and re-layouts  47.6 us (5%)
  between operations  16.4 us (2%)
    reduce_scatter x1, waiting for transfers between devices, on_device(): lax.psum_scatter(jnp.concatenate([jnp.einsum('rc,rk->ck', input_one, grad...  173 us
    all_gather x1, waiting for transfers between devices, move_task(): return jnp.sum(lax.all_gather(panel, net_axis), axis=0)  162 us
    reduce_scatter x1, waiting for transfers between devices, on_device(): lax.psum_scatter(key_terms, 'fsdp', scatter_dimension=1, tiled=True)  82.4 us
    psum x1, blocking collectives, on_device(): lax.psum((local_vectors[0], local_vectors[1], local_vectors[2], local_vec...  55 us
    all_gather x1, waiting for transfers between devices, on_device(): lax.all_gather(key_flat, 'fsdp', axis=1, tiled=True)  37.4 us
    unnamed x1, blocking collectives  26.5 us
    all_gather x1, waiting for transfers between devices, on_device(): lax.all_gather(value_flat, 'fsdp', axis=1, tiled=True)  23.9 us
    dot_general x1, matrix products, on_device(): jnp.einsum('sqhd,skhd->shqk', grad_heads, values, preferred_element_type=...  20.5 us
  transfers between devices with their start and end apart: 9, of which 5 were waited for; matrix products, arithmetic and copies ran while one was open for 29% of the time, Pallas kernels for 0%

profile of v1, /device:TPU:0, one launch (start us, length us, event | category | flops | bytes accessed | tf_op | source)
XLA Modules:
  0.0 892.7 jit_solution(17670693738919725443)
XLA Ops:
  8.7 1.3 convert_reduce_fusion.2
  10.1 1.5 fusion.28
  12.5 1.2 dynamic-slice
  15.1 0.8 dynamic-update-slice
  15.9 0.8 dynamic-update-slice.1
  16.8 0.8 dynamic-update-slice.3
  18.4 0.8 dynamic-update-slice.5
  19.3 0.8 dynamic-update-slice.6
  20.1 0.9 dynamic-update-slice.2
  21.0 26.5 %all-reduce.19 = (bf16[768]{0:T(1024)(128)(2,1)S(1)}, bf16[768]{0:T(1024)(128)(2,1)S(1)}, bf16[768]{0:T(1024)(128)(2,1)}, bf16[768]{0:T(1024)(128)(2,1)}, bf16[7...) all-reduce(bf16[768]{0:T(1024)(128)(2,1)S(1)} %dynamic-update-slice, ...), channel_id=1, replica_groups=mesh['rep'=4,'fsdp'=8] {'fsdp'}, use_global_device_ids=true, to_apply=%add.15 | all-reduce | flops 6912 | bytes 27648
  47.6 1.6 fusion.33
  49.2 6.1 convolution_add_fusion
  55.4 6.2 copy.46
  61.5 6.3 reshape.249
  67.9 2.2 fusion.78
  70.7 1.0 copy-done.7
  71.8 1.0 pad_maximum_fusion.3
  72.9 1.7 slice.108
  74.6 1.1 copy.47
  77.7 2.9 convolution_convert_fusion
  80.6 1.5 copy.51
  82.1 1.1 reshape.254
  83.2 1.4 slice.110
  84.6 37.4 %all-gather.14.cloned.1.call-done = bf16[4,1024,768]{1,2,0:T(8,128)(2,1)} async-done(((bf16[4,128,768]{1,2,0:T(8,128)(2,1)}), bf16[4,1024,768]{1,2,0:T(8,128)(2,1)}) %all-gather.14.cloned.1.call-update) | async-done | bytes 6291472 | tf_op jit(solution)/shard_map/all_gather | solution.py:132
  121.9 12.9 %select_reduce_fusion.1 = (f32[4,12,128]{2,1,0:T(8,128)S(1)}, f32[4,12,128,1024]{3,2,1,0:T(8,128)}) fusion(pred[4,128,1024]{2,1,0:T(8,128)(4,1)S(1)} %fusion.13, bf16[4,1024,12,64]{1,3,2,0:T(8,128)(2,1)} %bitcast.165, bf16[4,128,12,48]{1,3,2,0:T(8,128)(2,1)S(1)} %slice.110, bf16[4,128,12,16]{1,3,2,0:T(8,128)(2,1)S(1)} %get-tuple-element.61), kind=kOutput, calls=%fused_computation.6 | convolution fusion | flops 825747456 | bytes 32792576 | tf_op jit(solution)/shard_map/sqhd,skhd->shqk/dot_general | solution.py:115
  134.9 12.2 %select_reduce_fusion = f32[4,12,128]{2,1,0:T(8,128)S(1)} fusion(f32[4,12,128,1024]{3,2,1,0:T(8,128)} %get-tuple-element.76, f32[4,12,128]{2,1,0:T(8,128)S(1)} %broadcast_maximum_fusion, pred[4,128,1024]{2,1,0:T(8,128)(4,1)S(1)} %fusion.13), kind=kLoop, calls=%fused_computation.5 | loop fusion | flops 31451136 | bytes 25739264 | tf_op jit(solution)/shard_map/reduce_sum | solution.py:129
  147.1 23.9 %all-gather.12.cloned.1.call-done = bf16[4,1024,768]{1,2,0:T(8,128)(2,1)} async-done(((bf16[4,128,768]{1,2,0:T(8,128)(2,1)}), bf16[4,1024,768]{1,2,0:T(8,128)(2,1)}) %all-gather.12.cloned.1.call-update) | async-done | bytes 6291472 | tf_op jit(solution)/shard_map/all_gather | solution.py:133
  170.9 14.2 %fusion.58 = f32[4,12,64,128]{3,2,1,0:T(8,128)} fusion(bf16[4,1024,12,64]{1,3,2,0:T(8,128)(2,1)} %bitcast.192, f32[4,12,128,1024]{3,2,1,0:T(8,128)} %get-tuple-element.76, f32[4,12,128]{2,1,0:T(8,128)S(1)} %log_add_fusion, pred[4,128,1024]{2,1,0:T(8,128)(4,1)S(1)} %fusion.13), kind=kOutput, calls=%fused_computation.110 | convolution fusion | flops 830472192 | bytes 33579008 | tf_op jit(solution)/shard_map/shqk,skhd->sqhd/dot_general | solution.py:141
  185.2 15.0 %fusion.16 = f32[4,128,12]{1,2,0:T(8,128)S(1)} fusion(f32[4,12,64,128]{3,2,1,0:T(8,128)} %fusion.58, bf16[4,1024,12,64]{1,3,2,0:T(8,128)(2,1)} %bitcast.193, f32[4,12,128,1024]{3,2,1,0:T(8,128)} %get-tuple-element.76, f32[4,12,128]{2,1,0:T(8,128)S(1)} %log_add_fusion, pred[4,128,1024]{2,1,0:T(8,128)(4,1)S(1)} %fusion.13, bf16[4,128,12,64]{1,0,3,2:T(4,128)(2,1)} %reshape.254), kind=kOutput, calls=%fused_computation.48 | convolution fusion | flops 850913280 | bytes 34390016 | tf_op jit(solution)/shard_map/shqk,skhd->sqhd/dot_general | solution.py:142
  200.2 20.5 %multiply_convert_fusion = bf16[4,12,128,1024]{3,2,1,0:T(8,128)(2,1)} fusion(f32[4,12,128,1024]{3,2,1,0:T(8,128)} %get-tuple-element.76, f32[4,12,128]{2,1,0:T(8,128)S(1)} %bitcast.196, f32[4,12,128]{2,1,0:T(8,128)S(1)} %log_add_fusion, pred[4,128,1024]{2,1,0:T(8,128)(4,1)S(1)} %fusion.13, bf16[4,1024,12,64]{1,3,2,0:T(8,128)(2,1)} %bitcast.194, ...), kind=kOutput, calls=%fused_computation.2 | convolution fusion | flops 843055104 | bytes 45400064 | tf_op jit(solution)/shard_map/sqhd,skhd->shqk/dot_general | solution.py:180
  220.6 11.1 %fusion.50 = f32[4,12,64,1024]{3,2,1,0:T(8,128)} fusion(bf16[4,12,128,1024]{3,2,1,0:T(8,128)(2,1)} %multiply_convert_fusion, bf16[4,128,12,48]{1,3,2,0:T(8,128)(2,1)S(1)} %slice.110, bf16[4,128,12,16]{1,3,2,0:T(8,128)(2,1)S(1)} %get-tuple-element.61), kind=kOutput, calls=%fused_computation.98 | convolution fusion | flops 806879232 | bytes 25952256 | tf_op jit(solution)/shard_map/shqk,sqhd->skhd/dot_general | solution.py:187
  231.8 14.8 %fusion.47 = f32[4,12,64,1024]{3,2,1,0:T(8,128)} fusion(bf16[4,128,12,64]{1,0,3,2:T(4,128)(2,1)S(1)} %copy-done.12, f32[4,12,128,1024]{3,2,1,0:T(8,128)} %get-tuple-element.76, f32[4,12,128]{2,1,0:T(8,128)S(1)} %log_add_fusion, pred[4,128,1024]{2,1,0:T(8,128)(4,1)S(1)} %fusion.13), kind=kOutput, calls=%fused_computation.94 | convolution fusion | flops 830472192 | bytes 39084032 | tf_op jit(solution)/shard_map/shqk,sqhd->skhd/dot_general | solution.py:190
  246.5 18.8 %pad_maximum_fusion.1 = f32[4,1024,1536]{1,2,0:T(8,128)} fusion(f32[4,1024,768]{1,2,0:T(8,128)} %bitcast.164, f32[4,1024,768]{1,2,0:T(8,128)} %bitcast.163), kind=kLoop, calls=%fused_computation.1 | loop fusion | flops 6291456 | bytes 50331648 | tf_op jit(solution)/shard_map/concatenate | solution.py:193
  266.0 9.4 %all-gather.1 = bf16[8,1,384]{2,1,0:T(2,128)(2,1)S(1)} all-gather(bf16[1,1,384]{2,1,0:T(2,128)(2,1)S(1)} %reshape.281), channel_id=1, replica_groups=mesh['rep'=4,'fsdp'=8] {'fsdp'}, dimensions={0}, use_global_device_ids=true | all-gather | bytes 6912 | tf_op jit(solution)/shard_map/all_gather | solution.py:72
  275.5 1.2 fusion.31
  276.7 8.9 fusion.83
  285.6 19.4 %convert_reduce_fusion = (f32[3072]{0:T(1024)S(1)}, bf16[512,3072]{1,0:T(8,128)(2,1)S(1)}, f32[512,3072]{1,0:T(8,128)S(1)}) fusion(f32[512,3072]{1,0:T(8,128)} %fusion.83, f32[3072]{0:T(1024)S(1)} %bitcast.190, bf16[512,768]{1,0:T(8,128)(2,1)S(1)} %bitcast.172, bf16[768,3072]{1,0:T(8,128)(2,1)} %all-gather.20.cloned.1.call-done), kind=kOutput, calls=%fused_computation.12 | convolution fusion | flops 2533880832 | bytes 21258240 | tf_op jit(solution)/shard_map/dot_general | solution.py:163
  305.0 3.2 multiply_convert_fusion.1
  308.2 7.8 convolution_bitcast_fusion
  316.0 5.2 fusion.86
  321.2 11.3 %multiply_bitcast_fusion = f32[4,128,12,64]{1,3,2,0:T(8,128)S(1)} fusion(bf16[4,1024,12,64]{1,3,2,0:T(8,128)(2,1)} %bitcast.166, bf16[4,12,128,1024]{3,2,1,0:T(8,128)(2,1)} %multiply_convert_fusion), kind=kOutput, calls=%fused_computation.82 | convolution fusion | flops 805699584 | bytes 20447232 | tf_op jit(solution)/shard_map/shqk,skhd->sqhd/dot_general | solution.py:184
  332.5 2.3 convert_bitcast_fusion
  335.5 0.9 copy-done.9
  336.3 2.2 convolution_bitcast_fusion.1
  338.5 2.0 copy.57
  340.6 82.4 %reduce-scatter.3.cloned.1.call-done = f32[4,128,1536]{1,2,0:T(8,128)} async-done(((f32[4,1024,1536]{1,2,0:T(8,128)}), f32[4,128,1536]{1,2,0:T(8,128)}) %reduce-scatter.3.cloned.1.call-update) | async-done | bytes 3145744 | tf_op jit(solution)/shard_map/reduce_scatter | solution.py:200
  423.0 2.2 fusion.80
  427.4 2.2 copy.55
  429.7 1.5 copy-done.13
  431.2 4.9 fusion.9
  436.1 19.4 %pad_maximum_fusion = f32[768,9216]{1,0:T(8,128)} fusion(f32[768,3072]{1,0:T(8,128)} %convolution_bitcast_fusion, f32[768,3072]{1,0:T(8,128)} %fusion.86, f32[768,768]{1,0:T(8,128)S(1)} %copy.57, f32[768,2304]{1,0:T(8,128)} %fusion.9), kind=kLoop, calls=%fused_computation | loop fusion | flops 21233664 | bytes 56623104 | tf_op jit(solution)/shard_map/concatenate | solution.py:247
  455.8 173.1 %reduce-scatter.5.cloned.1.call-done = f32[96,9216]{1,0:T(8,128)} async-done(((f32[768,9216]{1,0:T(8,128)}), f32[96,9216]{1,0:T(8,128)}) %reduce-scatter.5.cloned.1.call-update) | async-done | bytes 3538960 | tf_op jit(solution)/shard_map/reduce_scatter | solution.py:246
  629.2 6.1 fusion.85
  635.3 5.7 fusion.84
  641.0 1.8 fusion.42
  642.9 5.7 fusion.76
  648.7 1.1 copy-done.6
  649.8 1.4 fusion.37
  651.2 55.0 %all-reduce.18 = (f32[768]{0:T(1024)S(1)}, f32[768]{0:T(1024)S(1)}, f32[768]{0:T(1024)S(1)}, f32[768]{0:T(1024)S(1)}, f32[2304]{0:T(1024)S(1)}, /*index=5*/f32[768]{0:T(1024)S(1)}, f32[3072]{0:T(1024)S(1)}) all-reduce(f32[768]{0:T(1024)S(1)} %get-tuple-element.23, ...), channel_id=1, replica_groups=mesh['rep'=4,'fsdp'=8] {'rep','fsdp'}, use_global_device_ids=true, to_apply=%region_13.14 | all-reduce | flops 9216 | bytes 73728 | tf_op jit(solution)/shard_map/psum | solution.py:228
  710.0 3.0 add_convert_fusion.2
  713.0 162.5 %all-gather.22.cloned.1.call-done = f32[384,9216]{1,0:T(8,128)} async-done(((f32[96,9216]{1,0:T(8,128)}), f32[384,9216]{1,0:T(8,128)}) %all-gather.22.cloned.1.call-update) | async-done | bytes 14155792 | tf_op jit(solution)/shard_map/all_gather | solution.py:15
  875.5 6.4 reduce_sum.156
  881.9 1.6 fusion.79
  883.5 1.0 slice.88
  (145 shorter events, 15.2 us)
Async XLA Ops:
  7.2 42.0 %all-gather.10.cloned.1.call-start = ((), (), s32[]{:S(2)}) async-start(), calls=%async_computation.2 | async-start | bytes 3981312 | tf_op jit(solution)/shard_map/all_gather | solution.py:84
  7.9 69.8 %all-gather.16.cloned.1.call-start = ((), (), s32[]{:S(2)}) async-start(), calls=%async_computation.5 | async-start | bytes 1327104 | tf_op jit(solution)/shard_map/all_gather | solution.py:146
  8.7 113.3 %all-gather.14.cloned.1.call-start = ((), (), s32[]{:S(2)}) async-start(), calls=%async_computation.4 | async-start | bytes 7077888 | tf_op jit(solution)/shard_map/all_gather | solution.py:132
  10.0 45.3 %copy-start.23 = (f32[512]{0:T(512)}, f32[512]{0:T(512)S(1)}, u32[]{:S(2)}) copy-start(f32[512]{0:T(512)S(1)} %get-tuple-element.73) | copy-start | bytes 6148
  11.6 263.9 %copy-start.27 = (f32[4,128]{1,0:T(4,128)}, f32[4,128]{1,0:T(4,128)S(1)}, u32[]{:S(2)}) copy-start(f32[4,128]{1,0:T(4,128)S(1)} %fusion.28) | copy-start | bytes 6148
  12.5 58.2 %copy-start.15 = (f32[4,128,16]{1,2,0:T(8,128)}, f32[4,128,16]{1,2,0:T(8,128)S(1)}, u32[]{:S(2)}) copy-start(f32[4,128,16]{1,2,0:T(8,128)S(1)} %get-tuple-element.67) | copy-start | bytes 98308
  12.5 58.2 %copy-start.17 = (f32[4,128,16]{1,2,0:T(8,128)}, f32[4,128,16]{1,2,0:T(8,128)S(1)}, u32[]{:S(2)}) copy-start(f32[4,128,16]{1,2,0:T(8,128)S(1)} %get-tuple-element.68) | copy-start | bytes 98308
  47.5 228.0 %copy-start.19 = (f32[768]{0:T(1024)}, f32[768]{0:T(1024)S(1)}, u32[]{:S(2)}) copy-start(f32[768]{0:T(1024)S(1)} %convert_element_type.126) | copy-start | bytes 9220
  47.5 7.9 copy-start.21
  47.6 7.8 copy-start.25
  70.5 1.2 copy-start.7
  71.7 6.0 copy-start.5
  72.8 98.1 %all-gather.12.cloned.1.call-start = ((), (), s32[]{:S(2)}) async-start(), calls=%async_computation.3 | async-start | bytes 7077888 | tf_op jit(solution)/shard_map/all_gather | solution.py:133
  75.6 201.1 %all-gather.18.cloned.1.call-start = ((), (), s32[]{:S(2)}) async-start(), calls=%async_computation.6 | async-start | bytes 5308416 | tf_op jit(solution)/shard_map/all_gather | solution.py:85
  76.2 209.3 %all-gather.20.cloned.1.call-start = ((), (), s32[]{:S(2)}) async-start(), calls=%async_computation.7 | async-start | bytes 5308416 | tf_op jit(solution)/shard_map/all_gather | solution.py:147
  76.8 346.2 %reduce-scatter.3.cloned.1.call-start = ((), (), s32[]{:S(2)}) async-start(), calls=%async_computation.8 | async-start | bytes 28311552 | tf_op jit(solution)/shard_map/reduce_scatter | solution.py:200
  220.6 11.1 %copy-start.12 = (bf16[4,128,12,64]{1,0,3,2:T(4,128)(2,1)S(1)}, bf16[4,128,12,64]{1,0,3,2:T(4,128)(2,1)}, u32[]{:S(2)}) copy-start(bf16[4,128,12,64]{1,0,3,2:T(4,128)(2,1)} %reshape.254) | copy-start | bytes 2359300
  265.3 0.7 copy-start.31
  265.3 10.1 %copy-start = (bf16[4,128,768]{2,1,0:T(8,128)(2,1)S(1)}, bf16[4,128,768]{2,1,0:T(8,128)(2,1)}, u32[]{:S(2)}) copy-start(bf16[4,128,768]{2,1,0:T(8,128)(2,1)} %param.15) | copy-start | bytes 2359300
  265.3 363.6 %reduce-scatter.5.cloned.1.call-start = ((), (), s32[]{:S(2)}) async-start(), calls=%async_computation.9 | async-start | bytes 31850496 | tf_op jit(solution)/shard_map/reduce_scatter | solution.py:246
  285.6 19.4 %copy-start.2 = (f32[512,3072]{1,0:T(8,128)S(1)}, f32[512,3072]{1,0:T(8,128)}, u32[]{:S(2)}) copy-start(f32[512,3072]{1,0:T(8,128)} %fusion.83) | copy-start | bytes 18874372
  305.0 11.0 %copy-start.8 = (bf16[512,3072]{1,0:T(8,128)(2,1)}, bf16[512,3072]{1,0:T(8,128)(2,1)S(1)}, u32[]{:S(2)}) copy-start(bf16[512,3072]{1,0:T(8,128)(2,1)S(1)} %get-tuple-element.39) | copy-start | bytes 9437188
  332.5 3.0 copy-start.3
  335.5 0.9 copy-start.9
  338.5 86.7 %copy-start.18 = (f32[4,128,16]{1,2,0:T(8,128)S(1)}, f32[4,128,16]{1,2,0:T(8,128)}, u32[]{:S(2)}) copy-start(f32[4,128,16]{1,2,0:T(8,128)} %copy-done.17) | copy-start | bytes 98308
  340.6 85.1 %copy-start.16 = (f32[4,128,16]{1,2,0:T(8,128)S(1)}, f32[4,128,16]{1,2,0:T(8,128)}, u32[]{:S(2)}) copy-start(f32[4,128,16]{1,2,0:T(8,128)} %copy-done.15) | copy-start | bytes 98308
  423.0 2.4 copy-start.4
  425.5 1.3 slice-start
  427.0 4.2 copy-start.14
  429.7 1.5 copy-start.13
  455.5 173.5 %copy-start.30 = (bf16[768]{0:T(1024)(128)(2,1)S(1)}, bf16[768]{0:T(1024)(128)(2,1)}, u32[]{:S(2)}) copy-start(bf16[768]{0:T(1024)(128)(2,1)} %get-tuple-element.34) | copy-start | bytes 4612
  455.5 173.5 %copy-start.29 = (bf16[768]{0:T(1024)(128)(2,1)S(1)}, bf16[768]{0:T(1024)(128)(2,1)}, u32[]{:S(2)}) copy-start(bf16[768]{0:T(1024)(128)(2,1)} %get-tuple-element.33) | copy-start | bytes 4612
  455.5 420.0 %all-gather.22.cloned.1.call-start = ((), (), s32[]{:S(2)}) async-start(), calls=%async_computation.10 | async-start | bytes 17694720 | tf_op jit(solution)/shard_map/all_gather | solution.py:15
  629.2 6.1 copy-start.11
  635.2 5.7 copy-start.1
  635.3 5.7 copy-start.10
  635.3 5.7 copy-start.32
  641.0 1.9 copy-start.20
  641.0 1.9 copy-start.22
  641.0 1.9 copy-start.24
  642.9 5.8 copy-start.28
  642.9 6.9 copy-start.26
  648.7 1.2 copy-start.6
  706.4 178.8 %copy-start.33 = (f32[96]{0:T(128)}, f32[96]{0:T(128)S(1)}, u32[]{:S(2)}) copy-start(f32[96]{0:T(128)S(1)} %dynamic_slice.26) | copy-start | bytes 1156
Sparse Core Ops, SparseCore 0:
  9.9 36.8 all-gather.9
  48.7 24.0 all-gather.15
  75.2 46.6 all-gather.13
  124.2 46.6 all-gather.11
  172.7 38.9 all-gather.17
  213.4 38.8 all-gather.19
  265.5 157.4 reduce-scatter.2
  455.7 173.2 reduce-scatter.4
  630.5 244.9 all-gather.21
